TPU v7x, 256 devices: a whole 4x4x8 slice. The times are simulated.
256 devices in a mesh: px: 32 (over z, y_lo, core), py: 8 (over x, y_hi).
Axes of the slice: x: 4, y: 4 (y_hi: 2, y_lo: 2; y = y_hi * 2 + y_lo), z: 8, core: 2. Of those that a mesh axis runs over, the one named last changes fastest.
Arguments:
- waves: float32 [2, 256, 131072], P(None, None, ('px', 'py')), may hold values from -6 to 6
- col_map: int32 [1024], P(('px', 'py')), may hold values from 0 to 63, as said below
- potential: float32 [128, 128, 128], P(None, 'px', 'py'), may hold values from -6 to 6
- projectors: float32 [2, 256, 131072], P(None, None, ('px', 'py')), may hold values from -0.1875 to 0.1875
- coupling: float32 [32, 8, 8], replicated, may hold values from -4 to 4
Outputs:
- hpsi: float32 [2, 16, 131072], P(None, None, ('px', 'py'))
- correlation: float32 [2, 256, 256], P(None, 'px', 'py')
- energy: float32 [2, 256, 16], P(None, 'px', 'py')
Inputs may be any that keep to these rules, and one draw needn't show every extreme that they name: `col_map`: on each device the 4 entries are distinct and ascending.
All inputs are finite; a program needn't handle non-finite values.
Results may differ from a plain program's by a relative error of at most 0.000064.
Values sent between devices are 32-bit elements; how exact they have to be, the bound alone decides.
A program may use at most 64 MiB of HBM per device.

v0:
```python
import math

import jax
import jax.numpy as jnp
from jax import lax
from jax.sharding import PartitionSpec as P

BW = 16
GCUT = 50


def frequency(index, length):
    return jnp.where(index < length // 2, index, index - length)


def dft_tables(rows_pos, cols_pos, length):
    product = rows_pos[:, None] * cols_pos[None, :] % length
    angle = product.astype(jnp.float32) * (2.0 * math.pi / length)
    factor = 1.0 / math.sqrt(length)
    return (jnp.cos(angle) * factor, jnp.sin(angle) * factor)


def line_dft(field, tables, sign, form):
    cosine, sine = tables
    highest = lax.Precision.HIGHEST
    real_cos = jnp.einsum(form, field[0], cosine, precision=highest)
    imag_cos = jnp.einsum(form, field[1], cosine, precision=highest)
    real_sin = jnp.einsum(form, field[0], sine, precision=highest)
    imag_sin = jnp.einsum(form, field[1], sine, precision=highest)
    return jnp.stack([real_cos - sign * imag_sin, imag_cos + sign * real_sin])


def block_of(matrix, row_start, rows, col_start, cols):
    return lax.dynamic_slice(matrix, (row_start * rows, col_start * cols), (rows, cols))


def body(waves, col_map, potential, projectors, coupling):
    highest = lax.Precision.HIGHEST
    px_count = lax.axis_size("px")
    py_count = lax.axis_size("py")
    row_index = lax.axis_index("px")
    col_index = lax.axis_index("py")
    ncold = col_map.shape[0]
    length = potential.shape[0]
    x_width = length // px_count
    y_width = length // py_count
    bands = waves.shape[1]
    natural_pos = jnp.arange(length, dtype=jnp.int32)
    x_order = natural_pos // x_width + px_count * (natural_pos % x_width)
    y_order = natural_pos // y_width + py_count * (natural_pos % y_width)
    z_inverse = dft_tables(natural_pos, natural_pos, length)
    y_inverse = dft_tables(y_order, natural_pos, length)
    x_inverse = dft_tables(x_order, natural_pos, length)
    y_forward = dft_tables(natural_pos, y_order, length)
    x_forward = dft_tables(natural_pos, x_order, length)
    x_global = row_index + px_count * (col_map // y_width)
    y_global = col_index + py_count * (col_map % y_width)
    freq_x = frequency(x_global, length)
    freq_y = frequency(y_global, length)
    freq_z = frequency(natural_pos, length)
    square = (freq_x * freq_x + freq_y * freq_y)[:, None] + (freq_z * freq_z)[None, :]
    sphere = jnp.where(square <= GCUT * GCUT, 1.0, 0.0).astype(jnp.float32).reshape(ncold * length)
    kinetic = (square.astype(jnp.float32) * (2.0 / (length * length))).reshape(ncold * length)
    masked = waves * sphere[None, None, :]
    beta = projectors * sphere[None, None, :]
    window = masked[:, :BW]
    columns = window.reshape(2, BW, ncold, length)
    slot_table = (
        jnp.arange(x_width * y_width, dtype=jnp.int32)[:, None] == col_map[None, :]
    ).astype(jnp.float32)
    slotted = jnp.einsum("sc,pbcz->pbsz", slot_table, columns, precision=highest).reshape(
        2, BW, x_width, y_width, length
    )
    zline = line_dft(slotted, z_inverse, 1.0, "bxyz,zk->bxyk")
    grid_rows = lax.all_to_all(zline, "py", split_axis=4, concat_axis=3, tiled=True)
    yline = line_dft(grid_rows, y_inverse, 1.0, "bxyz,yk->bxkz")
    pencils = lax.all_to_all(yline, "px", split_axis=3, concat_axis=2, tiled=True)
    real_space = line_dft(pencils, x_inverse, 1.0, "bxyz,xk->bkyz")
    weighted = real_space * potential[None, None]
    xback = line_dft(weighted, x_forward, -1.0, "bxyz,xk->bkyz")
    back_rows = lax.all_to_all(xback, "px", split_axis=2, concat_axis=3, tiled=True)
    yback = line_dft(back_rows, y_forward, -1.0, "bxyz,yk->bxkz")
    zrows = lax.all_to_all(yback, "py", split_axis=3, concat_axis=4, tiled=True)
    zback = line_dft(zrows, z_inverse, -1.0, "bxyz,zk->bxyk").reshape(
        2, BW, x_width * y_width, length
    )
    local = jnp.einsum("sc,pbsz->pbcz", slot_table, zback, precision=highest)
    local = local.reshape(2, BW, ncold * length)
    wave_re = window[0]
    wave_im = window[1]
    beta_re = beta[0]
    beta_im = beta[1]
    part_re = jnp.dot(beta_re, wave_re.T, precision=highest) + jnp.dot(
        beta_im, wave_im.T, precision=highest
    )
    part_im = jnp.dot(beta_re, wave_im.T, precision=highest) - jnp.dot(
        beta_im, wave_re.T, precision=highest
    )
    proj_re, proj_im = lax.psum((part_re, part_im), ("px", "py"))
    atoms = coupling.shape[0]
    block = coupling.shape[1]
    sym = 0.5 * (coupling + jnp.swapaxes(coupling, 1, 2))
    coef_re = jnp.einsum(
        "aij,ajb->aib", sym, proj_re.reshape(atoms, block, BW), precision=highest
    ).reshape(atoms * block, BW)
    coef_im = jnp.einsum(
        "aij,ajb->aib", sym, proj_im.reshape(atoms, block, BW), precision=highest
    ).reshape(atoms * block, BW)
    nonlocal_re = jnp.dot(coef_re.T, beta_re, precision=highest) - jnp.dot(
        coef_im.T, beta_im, precision=highest
    )
    nonlocal_im = jnp.dot(coef_im.T, beta_re, precision=highest) + jnp.dot(
        coef_re.T, beta_im, precision=highest
    )
    hpsi_re = kinetic[None, :] * wave_re + sphere[None, :] * local[0] + nonlocal_re
    hpsi_im = kinetic[None, :] * wave_im + sphere[None, :] * local[1] + nonlocal_im
    all_re = masked[0]
    all_im = masked[1]
    over_re = jnp.dot(all_re, all_re.T, precision=highest) + jnp.dot(
        all_im, all_im.T, precision=highest
    )
    over_im = jnp.dot(all_re, all_im.T, precision=highest) - jnp.dot(
        all_im, all_re.T, precision=highest
    )
    ham_re = jnp.dot(all_re, hpsi_re.T, precision=highest) + jnp.dot(
        all_im, hpsi_im.T, precision=highest
    )
    ham_im = jnp.dot(all_re, hpsi_im.T, precision=highest) - jnp.dot(
        all_im, hpsi_re.T, precision=highest
    )
    scale = 1.0 / (ncold * length * px_count * py_count)
    rows = bands // px_count
    over_cols = bands // py_count
    ham_cols = BW // py_count
    summed = lax.psum((over_re, over_im, ham_re, ham_im), ("px", "py"))
    own_over_re = block_of(summed[0], row_index, rows, col_index, over_cols)
    own_over_im = block_of(summed[1], row_index, rows, col_index, over_cols)
    own_ham_re = block_of(summed[2], row_index, rows, col_index, ham_cols)
    own_ham_im = block_of(summed[3], row_index, rows, col_index, ham_cols)
    hpsi = jnp.stack([hpsi_re, hpsi_im])
    correlation = jnp.stack([own_over_re, own_over_im]) * scale
    energy = jnp.stack([own_ham_re, own_ham_im]) * scale
    return (hpsi, correlation, energy)


def solution(mesh):
    placed = (
        P(None, None, ("px", "py")),
        P(("px", "py")),
        P(None, "px", "py"),
        P(None, None, ("px", "py")),
        P(),
    )
    return jax.shard_map(
        body,
        mesh=mesh,
        in_specs=placed,
        out_specs=(P(None, None, ("px", "py")), P(None, "px", "py"), P(None, "px", "py")),
        check_vma=False,
    )
```

profile of v0, /device:TPU:1, one launch (start us, length us, event | category | flops | bytes accessed | tf_op | source)
XLA Modules:
  0.0 595.4 jit_solution(16620383108514978220)
XLA Ops:
  8.0 1.8 broadcast_multiply_fusion.1
  14.1 6.3 %copy.44 = f32[2,16,4,16,128]{3,2,1,0,4:T(4,128)} copy(f32[2,16,4,16,128]{4,3,2,1,0:T(8,128)S(1)} %pad_maximum_fusion) | data formatting | bytes 2097152 | tf_op jit(solution)/shard_map/stack | solution.py:30
  20.4 10.1 %reshape.227 = f32[8,1,32768]{2,1,0:T(1,128)} reshape(f32[128,2,16,4,16]{4,3,2,1,0:T(4,128)} %bitcast.285) | data formatting | bytes 2097152
  30.5 7.6 %all-to-all-start = ((f32[8,1,32768]{2,1,0:T(1,128)}), f32[8,1,32768]{2,1,0:T(1,128)S(1)}, u32[]{:S(2)}, u32[]{:S(2)}) async-start(f32[8,1,32768]{2,1,0:T(1,128)} %reshape.227), calls=%async_computation | async-start | bytes 2097152 | tf_op jit(solution)/shard_map/all_to_all | solution.py:75
  38.2 15.3 %all-to-all-done = f32[8,1,32768]{2,1,0:T(1,128)S(1)} async-done(((f32[8,1,32768]{2,1,0:T(1,128)}), f32[8,1,32768]{2,1,0:T(1,128)S(1)}, u32[]{:S(2)}, u32[]{:S(2)}) %all-to-all-start) | async-done | bytes 1048608 | tf_op jit(solution)/shard_map/all_to_all | solution.py:75
  53.5 1.0 copy-done
  55.0 4.4 reduce
  59.4 9.0 %reshape.228 = f32[128,2,16,4,16]{4,3,2,1,0:T(4,128)} reshape(f32[8,32768]{1,0:T(8,128)S(1)} %reduce) | data formatting | bytes 2097152
  68.3 8.4 %copy.84 = f32[2,16,4,16,8,16]{3,4,5,2,1,0:T(8,128)S(1)} copy(f32[2,16,4,16,8,16]{3,2,1,0,5,4:T(4,128)} %bitcast.293) | data formatting | bytes 2097152 | tf_op jit(solution)/shard_map/all_to_all | solution.py:75
  76.8 3.8 fusion.277
  80.6 3.2 squeeze.75
  83.8 3.2 squeeze.76
  87.1 0.9 fusion.48
  88.0 0.9 fusion.46
  88.9 0.9 fusion.7
  89.8 0.9 fusion.6
  90.8 6.3 %copy.46 = f32[2,16,4,128,16]{4,2,1,0,3:T(4,128)} copy(f32[2,16,4,128,16]{3,4,2,1,0:T(8,128)S(1)} %pad_maximum_fusion.1) | data formatting | bytes 2097152 | tf_op jit(solution)/shard_map/stack | solution.py:30
  97.1 8.9 %reshape.229 = f32[32,1,8192]{2,1,0:T(1,128)} reshape(f32[128,2,16,4,16]{4,3,2,1,0:T(4,128)} %bitcast.286) | data formatting | bytes 2097152
  106.1 10.7 %all-to-all-start.1 = ((f32[32,1,8192]{2,1,0:T(1,128)}), f32[32,1,8192]{2,1,0:T(1,128)}, u32[]{:S(2)}, u32[]{:S(2)}) async-start(f32[32,1,8192]{2,1,0:T(1,128)} %reshape.229), calls=%async_computation.1 | async-start | bytes 2097152 | tf_op jit(solution)/shard_map/all_to_all | solution.py:77
  116.8 28.0 %all-to-all-done.1 = f32[32,1,8192]{2,1,0:T(1,128)} async-done(((f32[32,1,8192]{2,1,0:T(1,128)}), f32[32,1,8192]{2,1,0:T(1,128)}, u32[]{:S(2)}, u32[]{:S(2)}) %all-to-all-start.1) | async-done | bytes 1048608 | tf_op jit(solution)/shard_map/all_to_all | solution.py:77
  144.8 4.4 reduce.1
  149.2 7.2 %reshape.230 = f32[128,2,16,4,16]{4,3,2,1,0:T(4,128)} reshape(f32[32,8192]{1,0:T(8,128)S(1)} %reduce.1) | data formatting | bytes 2097152
  156.4 4.1 copy.47
  160.6 3.2 fusion.276
  163.8 2.3 copy.50
  166.1 3.7 copy.51
  169.8 0.9 fusion.82
  170.7 1.7 fusion.79
  172.4 4.7 copy.48
  177.2 3.9 copy.49
  181.1 0.9 fusion.80
  182.0 0.9 fusion.81
  182.9 1.2 add_bitcast_fusion.1
  187.9 6.3 %copy.54 = f32[2,16,128,4,16]{4,3,1,0,2:T(4,128)} copy(f32[2,16,128,4,16]{2,4,3,1,0:T(8,128)S(1)} %pad_maximum_fusion.2) | data formatting | bytes 2097152 | tf_op jit(solution)/shard_map/stack | solution.py:30
  194.2 8.9 %reshape.231 = f32[32,1,8192]{2,1,0:T(1,128)} reshape(f32[128,2,16,4,16]{4,3,2,1,0:T(4,128)} %bitcast.287) | data formatting | bytes 2097152
  203.1 5.5 all-to-all-start.2
  209.3 1.3 convolution_add_fusion.2
  211.2 1.3 convolution_subtract_fusion.2
  215.0 79.2 %all-reduce.1 = (f32[32,8,16]{2,1,0:T(8,128)}, f32[32,8,16]{2,1,0:T(8,128)S(1)}) all-reduce(f32[32,8,16]{2,1,0:T(8,128)S(1)} %bitcast.326, f32[32,8,16]{2,1,0:T(8,128)S(1)} %bitcast.325), channel_id=1, replica_groups=mesh['px'=32,'py'=8] {'px','py'}, use_global_device_ids=true, to_apply=%region_1.2 | all-reduce | flops 8192 | bytes 65536 | tf_op jit(solution)/shard_map/psum | solution.py:99
  294.2 4.4 reduce.2
  298.7 7.2 %reshape.232 = f32[128,2,16,4,16]{4,3,2,1,0:T(4,128)} reshape(f32[32,8192]{1,0:T(8,128)S(1)} %reduce.2) | data formatting | bytes 2097152
  305.9 4.7 copy.55
  310.6 3.2 fusion.275
  313.8 2.3 copy.56
  316.1 2.8 copy.57
  318.9 1.7 fusion.42
  320.6 4.7 copy.58
  325.3 2.8 copy.59
  329.0 1.9 fusion.5
  330.8 0.9 fusion.3
  331.8 6.3 %copy.62 = f32[2,16,4,128,16]{4,2,1,0,3:T(4,128)} copy(f32[2,16,4,128,16]{3,4,2,1,0:T(8,128)S(1)} %pad_maximum_fusion.3) | data formatting | bytes 2097152 | tf_op jit(solution)/shard_map/stack | solution.py:30
  338.1 10.2 %reshape.233 = f32[8,1,32768]{2,1,0:T(1,128)} reshape(f32[128,2,16,4,16]{4,3,2,1,0:T(4,128)} %bitcast.288) | data formatting | bytes 2097152
  348.3 4.4 all-to-all-start.3
  353.1 1.0 fusion.17
  354.8 112.4 %all-reduce.5.cloned.1.call-done = (f32[256,256]{1,0:T(8,128)}, f32[256,256]{1,0:T(8,128)}) async-done(((f32[256,256]{1,0:T(8,128)}, f32[256,256]{1,0:T(8,128)}), (f32[256,256]{1,0:T(8,128)}, f32[256,256]{1,0:T(8,128)})) %all-reduce.5.cloned.1.call-update) | async-done | bytes 524304 | tf_op jit(solution)/shard_map/psum | solution.py:135
  468.6 4.4 reduce.3
  473.0 9.0 %reshape.234 = f32[128,2,16,4,16]{4,3,2,1,0:T(4,128)} reshape(f32[8,32768]{1,0:T(8,128)S(1)} %reduce.3) | data formatting | bytes 2097152
  481.9 8.4 %copy.83 = f32[2,16,4,8,16,16]{5,3,4,2,1,0:T(8,128)S(1)} copy(f32[2,16,4,8,16,16]{5,2,1,0,4,3:T(4,128)} %bitcast.296) | data formatting | bytes 2097152 | tf_op jit(solution)/shard_map/all_to_all | solution.py:83
  490.4 3.8 fusion.274
  494.2 3.2 squeeze.83
  497.4 1.6 fusion.56
  499.0 3.2 squeeze.84
  503.1 1.9 fusion.1
  509.2 77.8 %all-reduce = (f32[256,16]{0,1:T(8,128)S(1)}, f32[256,16]{0,1:T(8,128)S(1)}) all-reduce(f32[256,16]{0,1:T(8,128)S(1)} %convolution_subtract_fusion.4, f32[256,16]{0,1:T(8,128)S(1)} %convolution_add_fusion.4), channel_id=1, replica_groups=mesh['px'=32,'py'=8] {'px','py'}, use_global_device_ids=true, to_apply=%region_5.6 | all-reduce | flops 8192 | bytes 65536 | tf_op jit(solution)/shard_map/psum | solution.py:135
  (71 shorter events, 22.7 us)
Async XLA Ops:
  7.2 2.7 copy-start.5
  30.5 23.0 %all-to-all-start = ((f32[8,1,32768]{2,1,0:T(1,128)}), f32[8,1,32768]{2,1,0:T(1,128)S(1)}, u32[]{:S(2)}, u32[]{:S(2)}) async-start(f32[8,1,32768]{2,1,0:T(1,128)} %reshape.227), calls=%async_computation | async-start | bytes 2097152 | tf_op jit(solution)/shard_map/all_to_all | solution.py:75
  53.5 1.0 copy-start
  106.1 38.7 %all-to-all-start.1 = ((f32[32,1,8192]{2,1,0:T(1,128)}), f32[32,1,8192]{2,1,0:T(1,128)}, u32[]{:S(2)}, u32[]{:S(2)}) async-start(f32[32,1,8192]{2,1,0:T(1,128)} %reshape.229), calls=%async_computation.1 | async-start | bytes 2097152 | tf_op jit(solution)/shard_map/all_to_all | solution.py:77
  177.2 6.9 %copy-start.3 = (f32[128,4,16]{0,2,1:T(8,128)S(1)}, f32[128,4,16]{0,2,1:T(8,128)}, u32[]{:S(2)}) copy-start(f32[128,4,16]{0,2,1:T(8,128)} %param.7) | copy-start | bytes 98308
  203.1 91.1 %all-to-all-start.2 = ((f32[32,1,8192]{2,1,0:T(1,128)}), f32[32,1,8192]{2,1,0:T(1,128)}, u32[]{:S(2)}, u32[]{:S(2)}) async-start(f32[32,1,8192]{2,1,0:T(1,128)} %reshape.231), calls=%async_computation.2 | async-start | bytes 2097152 | tf_op jit(solution)/shard_map/all_to_all | solution.py:81
  208.6 6.3 %copy-start.4 = (f32[32,8,8]{0,2,1:T(8,128)S(1)}, f32[32,8,8]{0,2,1:T(8,128)}, u32[]{:S(2)}) copy-start(f32[32,8,8]{0,2,1:T(8,128)} %param.9) | copy-start | bytes 24580
  208.6 258.6 %all-reduce.5.cloned.1.call-start = ((), (), s32[]{:S(2)}) async-start(), calls=%async_computation.4 | async-start | bytes 1048576 | tf_op jit(solution)/shard_map/psum | solution.py:135
  338.1 15.9 %copy-start.1 = (f32[32,8,16]{2,1,0:T(8,128)S(1)}, f32[32,8,16]{2,1,0:T(8,128)}, u32[]{:S(2)}) copy-start(f32[32,8,16]{2,1,0:T(8,128)} %get-tuple-element.5) | copy-start | bytes 49156
  348.3 120.3 %all-to-all-start.3 = ((f32[8,1,32768]{2,1,0:T(1,128)}), f32[8,1,32768]{2,1,0:T(1,128)}, u32[]{:S(2)}, u32[]{:S(2)}) async-start(f32[8,1,32768]{2,1,0:T(1,128)} %reshape.233), calls=%async_computation.3 | async-start | bytes 2097152 | tf_op jit(solution)/shard_map/all_to_all | solution.py:83
  499.0 7.3 %copy-start.2 = (f32[16,512]{1,0:T(8,128)S(1)}, f32[16,512]{1,0:T(8,128)}, u32[]{:S(2)}) copy-start(f32[16,512]{1,0:T(8,128)} %fusion.17) | copy-start | bytes 98308
Sparse Core Ops, SparseCore 0:
  215.1 252.1 all-reduce.4
where the time goes:
time: 602 us; the launch traced here: 595 us
  local copies, waits for them, and re-layouts  179 us (30%)
  blocking collectives  157 us (26%)
  waiting for transfers between devices  156 us (26%)
  matrix products  36.9 us (6%)
  starting transfers between devices  28.2 us (5%)
  other arithmetic  23.8 us (4%)
  between operations  14.8 us (2%)
    psum x1, waiting for transfers between devices, body(): summed = lax.psum((over_re, over_im, ham_re, ham_im), ('px', 'py'))  112 us
    psum x1, blocking collectives, body(): proj_re, proj_im = lax.psum((part_re, part_im), ('px', 'py'))  79.2 us
    psum x1, blocking collectives, body(): summed = lax.psum((over_re, over_im, ham_re, ham_im), ('px', 'py'))  77.8 us
    unnamed x20, local copies, waits for them, and re-layouts  71.5 us
    all_to_all x1, waiting for transfers between devices, body(): lax.all_to_all(yline, 'px', split_axis=3, concat_axis=2, tiled=True)  28 us
    another operation x4, local copies, waits for them, and re-layouts, line_dft(): return jnp.stack([real_cos - sign * imag_sin, imag_cos + sign * real_sin])  25.4 us
    slice x8, local copies, waits for them, and re-layouts, line_dft(): real_cos = jnp.einsum(form, field[0], cosine, precision=highest)  21.3 us
    all_to_all x1, waiting for transfers between devices, body(): lax.all_to_all(zline, 'py', split_axis=4, concat_axis=3, tiled=True)  15.3 us
  transfers between devices with their start and end apart: 5, of which 3 were waited for; matrix products, arithmetic and copies ran while one was open for 11% of the time, Pallas kernels for 0%

commit v1 on v0

v1 whole, which is shorter than its diff:
```python
import math

import jax
import jax.numpy as jnp
import numpy as np
from jax import lax
from jax.experimental import pallas as pl
from jax.experimental.pallas import tpu as pltpu
from jax.sharding import PartitionSpec as P

NG = 128
NB = 256
BW = 16
NCOLD = 4
GCUT = 50
NPX = 32
NPY = 8
NDEV = NPX * NPY
LOCAL = NCOLD * NG
MESH = pl.DeviceIdType.MESH
F32 = jnp.float32
BF16 = jnp.bfloat16


def dft_tables():
    index = np.arange(NG)
    angle = (index[:, None] * index[None, :] % NG) * (2.0 * math.pi / NG)
    cosine = np.cos(angle) / math.sqrt(NG)
    sine = np.sin(angle) / math.sqrt(NG)
    left = np.block([[cosine, -sine], [sine, cosine]])
    right = np.block([[cosine, sine], [-sine, cosine]])
    parts = []
    for table in (left, right):
        high = table.astype(jnp.bfloat16)
        low = (table - high.astype(np.float64)).astype(jnp.bfloat16)
        parts += [high, low]
    return np.stack(parts)


def split(x):
    high = x.astype(BF16)
    return high, (x - high.astype(F32)).astype(BF16)


def product(a, b, transposed=False):
    dims = (((1,), (1 if transposed else 0,)), ((), ()))

    def dot(u, v):
        return lax.dot_general(u, v, dims, preferred_element_type=F32)

    return dot(a[0], b[0]) + (dot(a[0], b[1]) + dot(a[1], b[0]))


def pair(ref, *index):
    return ref[(0, *index)], ref[(1, *index)]


def far_first(digit, half):
    odd = lax.rem(digit, 2)
    return half + (1 - 2 * odd) * lax.div(digit + 1, 2)


def partner_px(k, p):
    z = lax.rem(lax.div(p, 4) + far_first(lax.div(k, 4), 4), 8)
    y_lo = lax.rem(lax.div(p, 2) + 1 + lax.rem(lax.div(k, 2), 2), 2)
    core = lax.rem(p + 1 + lax.rem(k, 2), 2)
    return z * 4 + y_lo * 2 + core


def partner_py(k, q):
    x = lax.rem(lax.div(q, 2) + far_first(lax.div(k, 2), 2), 4)
    y_hi = lax.rem(q + 1 + lax.rem(k, 2), 2)
    return x * 2 + y_hi


def partner(k, p, q):
    p_digit = lax.div(k, 32) * 4 + lax.rem(k, 4)
    q_digit = lax.rem(lax.div(k, 4), 8)
    return partner_px(p_digit, p), partner_py(q_digit, q)


def remote(src, dst, sems, place):
    return pltpu.make_async_remote_copy(
        src_ref=src,
        dst_ref=dst,
        send_sem=sems.at[0],
        recv_sem=sems.at[1],
        device_id=place,
        device_id_type=MESH,
    )


def wait_bytes(ref, sem):
    pltpu.make_async_copy(ref, ref, sem).wait()


def kernel(
    waves_hbm,
    col_hbm,
    pot_hbm,
    beta_hbm,
    coup_hbm,
    mats_hbm,
    hpsi_ref,
    corr_ref,
    energy_ref,
    waves,
    beta,
    pot,
    coup,
    mats,
    col,
    phi_s,
    beta_s,
    sym_s,
    fwd_send,
    fwd_recv,
    pot_send,
    pot_recv,
    ca_send,
    ca_recv,
    cb_send,
    cb_recv,
    back_send,
    back_recv,
    en_send,
    en_recv,
    unpack,
    field,
    grid,
    picked,
    ham,
    load_sems,
    own_sems,
    fwd_sems,
    pot_sems,
    ca_sems,
    cb_sems,
    back_sems,
    en_sems,
):
    p = lax.axis_index("px")
    q = lax.axis_index("py")
    z_low = lax.div(p, 2)
    half = lax.rem(p, 2)
    owner = half * NG + q * 16 + z_low
    slot = q * NPX + p

    barrier = pltpu.get_barrier_semaphore()

    def greet(k, carry):
        pl.semaphore_signal(barrier, inc=1, device_id=partner(k, p, q), device_id_type=MESH)
        return carry

    loads = [
        (waves_hbm.at[:, pl.ds(0, BW)], waves.at[:, pl.ds(0, BW)]),
        (mats_hbm, mats),
        (col_hbm, col),
        (beta_hbm, beta),
        (waves_hbm.at[:, pl.ds(BW, NB - BW)], waves.at[:, pl.ds(BW, NB - BW)]),
        (pot_hbm, pot),
        (coup_hbm, coup),
    ]
    loads = [pltpu.make_async_copy(s, d, load_sems.at[i]) for i, (s, d) in enumerate(loads)]
    for load in loads:
        load.start()
    lax.fori_loop(0, NDEV - 1, greet, 0, unroll=5)

    lane = lax.broadcasted_iota(jnp.int32, (1, NG), 1)

    loads[0].wait()
    loads[1].wait()
    loads[2].wait()
    z_freq = jnp.where(lane < NG // 2, lane, lane - NG)
    spheres = []
    kinetics = []
    cols = jnp.zeros((1, NG), F32)
    for j in range(NCOLD):
        place = col[j]
        cols = jnp.where(lane == 96 + j, place.astype(F32), cols)
        x = p + NPX * lax.div(place, 16)
        y = q + NPY * lax.rem(place, 16)
        fx = jnp.where(x < NG // 2, x, x - NG)
        fy = jnp.where(y < NG // 2, y, y - NG)
        square = fx * fx + fy * fy + z_freq * z_freq
        spheres.append(jnp.where(square <= GCUT * GCUT, 1.0, 0.0).astype(F32))
        kinetics.append(square.astype(F32) * (2.0 / (NG * NG)))
    sphere = jnp.concatenate(spheres, axis=1)
    kinetic = jnp.concatenate(kinetics, axis=1)

    psi_re = waves[0, 0:BW, :] * sphere
    psi_im = waves[1, 0:BW, :] * sphere
    rows = []
    for h in range(2):
        for part in range(2):
            for j in range(NCOLD):
                re = psi_re[h * 8 : h * 8 + 8, j * NG : j * NG + NG]
                im = psi_im[h * 8 : h * 8 + 8, j * NG : j * NG + NG]
                rows.append(jnp.concatenate([re, -im] if part == 0 else [im, re], axis=1))
    z_rows = product(pair(mats.at[pl.ds(2, 2)], slice(0, NG)), split(jnp.concatenate(rows)), True)

    loads[3].wait()
    for part in range(2):
        high, low = split(beta[part] * sphere)
        beta_s[0, part * NB : part * NB + NB, :] = high
        beta_s[1, part * NB : part * NB + NB, :] = low
    zeros = jnp.zeros((32, LOCAL), F32)
    with_re = split(jnp.concatenate([zeros, zeros, psi_re, psi_im, zeros]))
    with_im = split(jnp.concatenate([zeros, zeros, psi_im, -psi_re, zeros]))
    partial = product(pair(beta_s, slice(0, NB)), with_re, True) + product(
        pair(beta_s, slice(NB, 2 * NB)), with_im, True
    )
    for h in range(2):
        part = pltpu.roll(z_rows, 64, 1) if h else z_rows
        rows = jnp.where(lane < 64, part, partial[h * NG : h * NG + NG]) + cols
        fwd_send[h * NG : h * NG + NG, 0, :] = rows

    loads[5].wait()
    for y in range(4):
        pot_send[:, y, :] = pot[:, y, :].T

    pl.semaphore_wait(barrier, NDEV - 1)

    def send_forward(k, carry):
        to_p, to_q = partner(k, p, q)
        row = lax.rem(to_p, 2) * NG + to_q * 16 + lax.div(to_p, 2)
        remote(fwd_send.at[row], fwd_recv.at[slot], fwd_sems, (to_p, to_q)).start()
        return carry

    lax.fori_loop(0, NDEV - 1, send_forward, 0, unroll=5)
    own_forward = pltpu.make_async_copy(fwd_send.at[owner], fwd_recv.at[slot], own_sems.at[0])
    own_forward.start()

    def send_potential(k, carry):
        to_p = partner_px(k, p)
        remote(pot_send.at[lax.div(to_p, 2)], pot_recv.at[p], pot_sems, (to_p, q)).start()
        return carry

    lax.fori_loop(0, NPX - 1, send_potential, 0)
    own_pot = pltpu.make_async_copy(pot_send.at[z_low], pot_recv.at[p], own_sems.at[1])
    own_pot.start()

    loads[4].wait()
    for part in range(2):
        high, low = split(waves[part] * sphere)
        phi_s[0, :, part * LOCAL : part * LOCAL + LOCAL] = high
        phi_s[1, :, part * LOCAL : part * LOCAL + LOCAL] = low
    phi = pair(phi_s)
    turned = tuple(jnp.concatenate([-x[:, LOCAL:], x[:, :LOCAL]], axis=1) for x in phi)
    ca_send[:, 0] = product(phi, phi, True).reshape(NPY, 32, NB)
    ca_send[:, 1] = product(phi, turned, True).reshape(NPY, 32, NB)

    def send_corr_a(k, carry):
        to_q = partner_py(k, q)
        remote(ca_send.at[to_q], ca_recv.at[q], ca_sems, (p, to_q)).start()
        return carry

    lax.fori_loop(0, NPY - 1, send_corr_a, 0)
    own_ca = pltpu.make_async_copy(ca_send.at[q], ca_recv.at[q], own_sems.at[2])
    own_ca.start()

    loads[6].wait()
    blk_row = lax.broadcasted_iota(jnp.int32, (8, NB), 0)
    blk_lane = lax.broadcasted_iota(jnp.int32, (8, NB), 1)
    spread = jnp.where(lax.rem(blk_lane, 8) == blk_row, 1.0, 0.0).astype(F32)
    wide = jnp.dot(coup[...], spread, precision=lax.Precision.HIGHEST, preferred_element_type=F32)
    sym_row = lax.broadcasted_iota(jnp.int32, (NB, NB), 0)
    sym_lane = lax.broadcasted_iota(jnp.int32, (NB, NB), 1)
    wide = jnp.where(lax.div(sym_row, 8) == lax.div(sym_lane, 8), wide, 0.0)
    high, low = split(0.5 * (wide + wide.T))
    sym_s[0] = high
    sym_s[1] = low
    picked[...] = jnp.zeros((NPY * NG, NG), F32)

    own_forward.wait()
    wait_bytes(fwd_recv.at[pl.ds(0, NDEV - 1)], fwd_sems.at[1])
    proj_sum = jnp.zeros((NPX, NG), F32)
    for s in range(NPY):
        block = fwd_recv[s * NPX : s * NPX + NPX, 0, :]
        proj_sum = proj_sum + block
        unpack[s * NG : s * NG + NG, :] = jnp.concatenate([block] * 4).T
    proj_sum = jnp.sum(proj_sum, axis=0, keepdims=True)
    proj_row = jnp.where((lane >= 64) & (lane < 96), proj_sum, 0.0)
    x_slot = lax.div(lane, 32).astype(F32) * 16.0
    y_slot = lax.broadcasted_iota(jnp.int32, (16, NPY, NG), 0).astype(F32)
    found = []
    for j in range(NCOLD):
        place = unpack[pl.ds(96 + j, NPY, stride=NG), :] - x_slot
        found.append(y_slot == place[None])
    for b in range(8):
        for part in range(2):
            plane = jnp.zeros((16, NPY, NG), F32)
            for j in range(NCOLD):
                value = unpack[pl.ds(part * 32 + j * 8 + b, NPY, stride=NG), :]
                plane = jnp.where(found[j], value[None], plane)
            field[part * NG : part * NG + NG, b * NG : b * NG + NG] = plane.reshape(NG, NG)

    own_pot.wait()
    wait_bytes(pot_recv.at[pl.ds(0, NPX - 1)], pot_sems.at[1])
    potential = pot_recv[...].reshape(NG, NG)
    potential = jnp.concatenate([potential, potential], axis=1)
    mat_a = pair(mats.at[pl.ds(0, 2)])
    mat_b = pair(mats.at[pl.ds(2, 2)])
    for c in range(4):
        two = slice(c * 256, c * 256 + 256)
        lines = product(mat_a, split(field[:, two]))
        planes = []
        for b in range(2):
            part = lines[:, b * NG : b * NG + NG]
            planes.append(jnp.concatenate([part[:NG], part[NG:]], axis=1))
        real = product(split(jnp.concatenate(planes)), mat_b)
        real = real * jnp.concatenate([potential, potential])
        back = product(split(real), mat_a)
        columns = []
        for b in range(2):
            part = back[b * NG : b * NG + NG]
            columns.append(jnp.concatenate([part[:, :NG], part[:, NG:]]))
        grid[:, two] = product(mat_b, split(jnp.concatenate(columns, axis=1)))
    for b in range(8):
        for part in range(2):
            plane = grid[part * NG : part * NG + NG, b * NG : b * NG + NG].reshape(16, NPY, NG)
            for j in range(NCOLD):
                value = jnp.sum(jnp.where(found[j], plane, 0.0), axis=0)
                picked[pl.ds(part * 32 + j * 8 + b, NPY, stride=NG), :] = value
    for s in range(NPY):
        turned = picked[s * NG : s * NG + NG, :].T
        block = turned[0:32] + turned[32:64] + turned[64:96] + turned[96:128]
        back_send[s * NPX : s * NPX + NPX, 0, :] = block + proj_row

    def send_back(k, carry):
        to_p, to_q = partner(k, p, q)
        remote(
            back_send.at[to_q * NPX + to_p], back_recv.at[owner], back_sems, (to_p, to_q)
        ).start()
        return carry

    lax.fori_loop(0, NDEV - 1, send_back, 0, unroll=5)
    own_back = pltpu.make_async_copy(back_send.at[slot], back_recv.at[owner], own_sems.at[3])
    own_back.start()

    own_ca.wait()
    wait_bytes(ca_recv.at[pl.ds(0, NPY - 1)], ca_sems.at[1])
    total = ca_recv[0]
    for s in range(1, NPY):
        total = total + ca_recv[s]
    total = total.reshape(64, NB)
    total = jnp.concatenate([total, jnp.zeros((64, NB), F32)])
    cb_send[...] = total.T.reshape(NPX, 8, NG)

    def send_corr_b(k, carry):
        to_p = partner_px(k, p)
        remote(cb_send.at[to_p], cb_recv.at[p], cb_sems, (to_p, q)).start()
        return carry

    lax.fori_loop(0, NPX - 1, send_corr_b, 0)
    own_cb = pltpu.make_async_copy(cb_send.at[p], cb_recv.at[p], own_sems.at[4])
    own_cb.start()

    own_back.wait()
    wait_bytes(back_recv.at[pl.ds(0, NDEV - 1)], back_sems.at[1])
    low_rows = back_recv[0:NG, 0, :]
    high_rows = back_recv[NG : 2 * NG, 0, :]
    lines = jnp.where(lane < 64, low_rows, pltpu.roll(high_rows, 64, 1)).T
    lines = product(split(lines), pair(mats.at[pl.ds(2, 2)], slice(0, NG)))
    local_re = []
    local_im = []
    for h in range(2):
        res = [lines[h * 64 + j * 8 : h * 64 + j * 8 + 8] for j in range(4)]
        ims = [lines[h * 64 + 32 + j * 8 : h * 64 + 40 + j * 8] for j in range(4)]
        local_re.append(
            jnp.concatenate([r[:, :NG] + i[:, NG:] for r, i in zip(res, ims)], axis=1)
        )
        local_im.append(
            jnp.concatenate([i[:, :NG] - r[:, NG:] for r, i in zip(res, ims)], axis=1)
        )

    proj = jnp.concatenate([low_rows, high_rows])
    proj = pltpu.roll(proj, 64, 1).T[0:32]
    coef = product(split(proj), pair(sym_s))
    coef_re = coef[0:16]
    coef_im = coef[16:32]
    coef = jnp.concatenate(
        [
            jnp.concatenate([coef_re, -coef_im], axis=1),
            jnp.concatenate([coef_im, coef_re], axis=1),
        ]
    )
    nonlocal_part = product(split(coef), pair(beta_s))
    psi_re = waves[0, 0:BW, :] * sphere
    psi_im = waves[1, 0:BW, :] * sphere
    hpsi_re = kinetic * psi_re + sphere * jnp.concatenate(local_re) + nonlocal_part[0:16]
    hpsi_im = kinetic * psi_im + sphere * jnp.concatenate(local_im) + nonlocal_part[16:32]
    hpsi_ref[0] = hpsi_re
    hpsi_ref[1] = hpsi_im

    rows = []
    for h in range(2):
        re = hpsi_re[h * 8 : h * 8 + 8]
        im = hpsi_im[h * 8 : h * 8 + 8]
        rows.append(jnp.concatenate([re, im], axis=1))
        rows.append(jnp.concatenate([im, -re], axis=1))
    rows = split(jnp.concatenate(rows))
    rows = tuple(jnp.concatenate([x[0:16]] * 8 + [x[16:32]] * 8) for x in rows)
    partial = product(pair(phi_s), rows, True)
    for h in range(2):
        ham[...] = partial[:, h * NG : h * NG + NG]
        block = jnp.zeros((NPX, NG), F32)
        for m in range(8):
            strip = ham[pl.ds(m, NPX, stride=8), :]
            block = jnp.where(lax.div(lane, 16) == m, strip, block)
        en_send[h * NPX : h * NPX + NPX, 0, :] = block

    def send_energy(k, carry):
        to_p, to_q = partner(k, p, q)
        remote(
            en_send.at[lax.div(to_q, 4) * NPX + to_p], en_recv.at[slot], en_sems, (to_p, to_q)
        ).start()
        return carry

    lax.fori_loop(0, NDEV - 1, send_energy, 0, unroll=5)
    own_en = pltpu.make_async_copy(
        en_send.at[lax.div(q, 4) * NPX + p], en_recv.at[slot], own_sems.at[5]
    )
    own_en.start()

    scale = 1.0 / (NDEV * LOCAL)
    own_cb.wait()
    wait_bytes(cb_recv.at[pl.ds(0, NPX - 1)], cb_sems.at[1])
    total = jnp.sum(cb_recv[...], axis=0) * scale
    corr_ref[0] = total[:, 0:32]
    corr_ref[1] = total[:, 32:64]

    own_en.wait()
    wait_bytes(en_recv.at[pl.ds(0, NDEV - 1)], en_sems.at[1])
    total = jnp.zeros((NPX, NG), F32)
    for s in range(NPY):
        total = total + en_recv[s * NPX : s * NPX + NPX, 0, :]
    total = jnp.sum(total, axis=0, keepdims=True) * scale
    m_row = lax.broadcasted_iota(jnp.int32, (8, NG), 0)
    m_lane = lax.broadcasted_iota(jnp.int32, (8, NG), 1)
    mine = jnp.where(lax.div(m_lane, 16) == m_row, total, 0.0)
    for part in range(2):
        n_first = part * 8 + lax.rem(q, 4) * 2
        for n in range(2):
            one = jnp.where(lax.rem(m_lane, 16) == n_first + n, mine, 0.0)
            energy_ref[part, :, n : n + 1] = jnp.sum(one, axis=1, keepdims=True)

    wait_bytes(fwd_send.at[pl.ds(0, NDEV - 1)], fwd_sems.at[0])
    wait_bytes(pot_recv.at[pl.ds(0, NPX - 1)], pot_sems.at[0])
    wait_bytes(ca_send.at[pl.ds(0, NPY - 1)], ca_sems.at[0])
    wait_bytes(cb_send.at[pl.ds(0, NPX - 1)], cb_sems.at[0])
    wait_bytes(back_send.at[pl.ds(0, NDEV - 1)], back_sems.at[0])
    wait_bytes(en_recv.at[pl.ds(0, NDEV - 1)], en_sems.at[0])


def body(waves, col_map, potential, projectors, coupling):
    vmem = pltpu.VMEM
    anywhere = pl.BlockSpec(memory_space=pl.ANY)
    inside = pl.BlockSpec(memory_space=pltpu.VMEM)
    mats = jnp.asarray(dft_tables())
    return pl.pallas_call(
        kernel,
        out_shape=(
            jax.ShapeDtypeStruct((2, BW, LOCAL), F32),
            jax.ShapeDtypeStruct((2, 8, 32), F32),
            jax.ShapeDtypeStruct((2, 8, 2), F32),
        ),
        in_specs=[anywhere] * 6,
        out_specs=(inside, inside, inside),
        scratch_shapes=[
            vmem((2, NB, LOCAL), F32),
            vmem((2, NB, LOCAL), F32),
            vmem((NG, 4, 16), F32),
            vmem((NB, 8), F32),
            vmem((4, 256, 256), BF16),
            pltpu.SMEM((NCOLD,), jnp.int32),
            vmem((2, NB, 2 * LOCAL), BF16),
            vmem((2, 2 * NB, LOCAL), BF16),
            vmem((2, NB, NB), BF16),
            vmem((NDEV, 1, NG), F32),
            vmem((NDEV, 1, NG), F32),
            vmem((16, 4, NG), F32),
            vmem((NPX, 4, NG), F32),
            vmem((NPY, 2, 32, NB), F32),
            vmem((NPY, 2, 32, NB), F32),
            vmem((NPX, 8, NG), F32),
            vmem((NPX, 8, NG), F32),
            vmem((NDEV, 1, NG), F32),
            vmem((NDEV, 1, NG), F32),
            vmem((2 * NPX, 1, NG), F32),
            vmem((NDEV, 1, NG), F32),
            vmem((NPY * NG, NG), F32),
            vmem((2 * NG, 8 * NG), F32),
            vmem((2 * NG, 8 * NG), F32),
            vmem((NPY * NG, NG), F32),
            vmem((NB, NG), F32),
            pltpu.SemaphoreType.DMA((7,)),
            pltpu.SemaphoreType.DMA((6,)),
            pltpu.SemaphoreType.DMA((2,)),
            pltpu.SemaphoreType.DMA((2,)),
            pltpu.SemaphoreType.DMA((2,)),
            pltpu.SemaphoreType.DMA((2,)),
            pltpu.SemaphoreType.DMA((2,)),
            pltpu.SemaphoreType.DMA((2,)),
        ],
        compiler_params=pltpu.CompilerParams(
            collective_id=0, has_side_effects=True, vmem_limit_bytes=40 << 20
        ),
        name="hamiltonian",
    )(waves, col_map, potential, projectors, coupling.reshape(NB, 8), mats)


def solution(mesh):
    placed = (
        P(None, None, ("px", "py")),
        P(("px", "py")),
        P(None, "px", "py"),
        P(None, None, ("px", "py")),
        P(),
    )
    return jax.shard_map(
        body,
        mesh=mesh,
        in_specs=placed,
        out_specs=(P(None, None, ("px", "py")), P(None, "px", "py"), P(None, "px", "py")),
        check_vma=False,
    )
```

time: 602 us -> 77.9 us (0.13); the launches traced: 595 us -> 77.7 us
  local copies, waits for them, and re-layouts: 179 us -> 6.89 us
  blocking collectives: 157 us -> 0 us
  waiting for transfers between devices: 156 us -> 0 us
  Pallas kernels: 0 us -> 70.1 us
  matrix products: 36.9 us -> 0 us
  starting transfers between devices: 28.2 us -> 0 us
  other arithmetic: 23.8 us -> 0 us
  between operations: 14.8 us -> 0.68 us
    psum x2 -> x0, blocking collectives: 157 us -> none  [the longest x1 79.2 us: body(): proj_re, proj_im = lax.psum((part_re, part_im), ('px', 'py'))]
    psum x1 -> x0, waiting for transfers between devices: 112 us -> none  [body(): summed = lax.psum((over_re, over_im, ham_re, ham_im), ('px', 'py'))]
    pallas_call x0 -> x1, Pallas kernels: none -> 70.1 us  [body(): pl.pallas_call(kernel, out_shape=(jax.ShapeDtypeStruct((2, BW, LOCAL), F3...]
    unnamed x20 -> x14, local copies, waits for them, and re-layouts: 71.5 us -> 6.23 us
    all_to_all x4 -> x0, waiting for transfers between devices: 43.3 us -> none  [the longest x1 28 us: body(): lax.all_to_all(yline, 'px', split_axis=3, concat_axis=2, tiled=True)]
    dot_general x36 -> x0, matrix products: 29.2 us -> none  [the longest x4 5.46 us: line_dft(): imag_sin = jnp.einsum(form, field[1], sine, precision=highest)]
    slice x12 -> x0, local copies, waits for them, and re-layouts: 28.3 us -> none  [the longest x8 21.3 us: line_dft(): real_cos = jnp.einsum(form, field[0], cosine, precision=highest)]
    all_to_all x4 -> x0, starting transfers between devices: 28.2 us -> none  [the longest x1 10.7 us: body(): lax.all_to_all(yline, 'px', split_axis=3, concat_axis=2, tiled=True)]
  transfers between devices with their start and end apart: 5 -> 0, of which waited for: 3 -> 0; matrix products, arithmetic and copies ran while one was open for 11% -> 0% of each run, Pallas kernels for 0% -> 0%
where the time goes in v1:
time: 77.9 us; the launch traced here: 77.7 us
  Pallas kernels  70.1 us (90%)
  local copies, waits for them, and re-layouts  6.89 us (9%)
    pallas_call x1, Pallas kernels, body(): pl.pallas_call(kernel, out_shape=(jax.ShapeDtypeStruct((2, BW, LOCAL), F3...  70.1 us
    unnamed x14, local copies, waits for them, and re-layouts  6.23 us

profile of v1, /device:TPU:1, one launch (start us, length us, event | category | flops | bytes accessed | tf_op | source)
XLA Modules:
  0.0 77.7 jit_solution(16112963668052709016)
XLA Ops:
  0.6 0.0 copy-start.4
  0.6 0.9 %copy.9 = f32[32,8,8]{2,1,0:T(8,128)S(1)} copy(f32[32,8,8]{0,2,1:T(8,128)} %param.10) | data formatting | bytes 16384 | tf_op args[4]
  1.5 0.0 copy-done.4
  1.5 0.0 copy-start.3
  1.5 0.1 copy.10.pot_hbm
  1.7 0.5 copy-done.3
  2.2 0.0 copy-start
  2.2 1.2 %copy-done = f32[2,256,512]{2,1,0:T(8,128)S(1)} copy-done((f32[2,256,512]{2,1,0:T(8,128)S(1)}, f32[2,256,512]{2,1,0:T(8,128)}, u32[]{:S(2)}) %copy-start) | copy-done | bytes 1048600
  3.4 0.0 copy-start.1
  3.4 1.2 %copy-done.1 = f32[2,256,512]{2,1,0:T(8,128)S(1)} copy-done((f32[2,256,512]{2,1,0:T(8,128)S(1)}, f32[2,256,512]{2,1,0:T(8,128)}, u32[]{:S(2)}) %copy-start.1) | copy-done | bytes 1048600
  4.6 0.0 copy-start.2
  4.6 1.0 %copy-done.2 = bf16[4,256,256]{2,1,0:T(8,128)(2,1)S(1)} copy-done((bf16[4,256,256]{2,1,0:T(8,128)(2,1)S(1)}, bf16[4,256,256]{2,1,0:T(8,128)(2,1)}, u32[]{:S(2)}) %copy-start.2) | copy-done | bytes 524312
  5.7 70.1 %hamiltonian.1 = (f32[2,16,512]{2,1,0:T(8,128)S(1)}, f32[2,8,32]{2,1,0:T(8,128)S(1)}, f32[2,8,2]{2,1,0:T(8,128)S(1)}) custom-call(f32[2,256,512]{2,1,0:T(8,128)S(1)} %copy-done, s32[4]{0:T(128)S(1)} %copy-done.3, f32[128,4,16]{2,1,0:T(4,128)S(1)} %copy.10.pot_hbm, f32[2,256,512]{2,1,0:T(8,128)S(1)} %copy-done.1, f32[256,8]{1,0:T(8,128)S(1)} %bitcast.1, ...), custom_call_target="tpu_custom_call" | custom-call | tf_op jit(solution)/shard_map/hamiltonian/pallas_call | solution.py:461
  75.8 0.7 copy.11
  76.4 0.6 copy.14
  77.1 0.6 copy.15
Async XLA Ops:
  0.6 0.9 %copy-start.4 = (f32[128,4,16]{0,2,1:T(8,128)S(1)}, f32[128,4,16]{0,2,1:T(8,128)}, u32[]{:S(2)}) copy-start(f32[128,4,16]{0,2,1:T(8,128)} %param.8) | copy-start | bytes 98308
  1.5 0.7 copy-start.3
  2.2 1.2 %copy-start = (f32[2,256,512]{2,1,0:T(8,128)S(1)}, f32[2,256,512]{2,1,0:T(8,128)}, u32[]{:S(2)}) copy-start(f32[2,256,512]{2,1,0:T(8,128)} %waves_hbm.1) | copy-start | bytes 3145732
  3.4 1.2 %copy-start.1 = (f32[2,256,512]{2,1,0:T(8,128)S(1)}, f32[2,256,512]{2,1,0:T(8,128)}, u32[]{:S(2)}) copy-start(f32[2,256,512]{2,1,0:T(8,128)} %beta_hbm.1) | copy-start | bytes 3145732
  4.6 1.0 %copy-start.2 = (bf16[4,256,256]{2,1,0:T(8,128)(2,1)S(1)}, bf16[4,256,256]{2,1,0:T(8,128)(2,1)}, u32[]{:S(2)}) copy-start(bf16[4,256,256]{2,1,0:T(8,128)(2,1)} %constant.2.clone.mats_hbm) | copy-start | bytes 1572868

commit v2 on v1

--- a/solution.py
+++ b/solution.py
@@ -25,16 +25,7 @@
 def dft_tables():
     index = np.arange(NG)
     angle = (index[:, None] * index[None, :] % NG) * (2.0 * math.pi / NG)
-    cosine = np.cos(angle) / math.sqrt(NG)
-    sine = np.sin(angle) / math.sqrt(NG)
-    left = np.block([[cosine, -sine], [sine, cosine]])
-    right = np.block([[cosine, sine], [-sine, cosine]])
-    parts = []
-    for table in (left, right):
-        high = table.astype(jnp.bfloat16)
-        low = (table - high.astype(np.float64)).astype(jnp.bfloat16)
-        parts += [high, low]
-    return np.stack(parts)
+    return np.stack([np.cos(angle), np.sin(angle)]).astype(np.float32) / np.float32(math.sqrt(NG))
 
 
 def split(x):
@@ -73,10 +64,24 @@
     return x * 2 + y_hi
 
 
-def partner(k, p, q):
-    p_digit = lax.div(k, 32) * 4 + lax.rem(k, 4)
-    q_digit = lax.rem(lax.div(k, 4), 8)
-    return partner_px(p_digit, p), partner_py(q_digit, q)
+def each_other(p, q, visit):
+    z = lax.div(p, 4)
+    y_lo = lax.rem(lax.div(p, 2), 2)
+    core = lax.rem(p, 2)
+    near = [(1 - y_lo, 1 - core), (1 - y_lo, core), (y_lo, 1 - core), (y_lo, core)]
+    across = [partner_py(jnp.int32(k), q) for k in range(NPY)]
+
+    def level(digit, carry):
+        to_z = lax.rem(z + far_first(digit, 4), 8)
+        for to_q in across:
+            for to_y, to_core in near:
+                visit(to_z, to_y, to_core, to_q)
+        return carry
+
+    lax.fori_loop(0, 7, level, 0)
+    others = [(to_y, to_core, to_q) for to_q in across for to_y, to_core in near]
+    for to_y, to_core, to_q in others[:-1]:
+        visit(z, to_y, to_core, to_q)
 
 
 def remote(src, dst, sems, place):
@@ -108,6 +113,7 @@
     beta,
     pot,
     coup,
+    tables,
     mats,
     col,
     phi_s,
@@ -148,13 +154,13 @@
 
     barrier = pltpu.get_barrier_semaphore()
 
-    def greet(k, carry):
-        pl.semaphore_signal(barrier, inc=1, device_id=partner(k, p, q), device_id_type=MESH)
-        return carry
+    def greet(to_z, to_y, to_core, to_q):
+        to_p = to_z * 4 + (to_y * 2 + to_core)
+        pl.semaphore_signal(barrier, inc=1, device_id=(to_p, to_q), device_id_type=MESH)
 
     loads = [
         (waves_hbm.at[:, pl.ds(0, BW)], waves.at[:, pl.ds(0, BW)]),
-        (mats_hbm, mats),
+        (mats_hbm, tables),
         (col_hbm, col),
         (beta_hbm, beta),
         (waves_hbm.at[:, pl.ds(BW, NB - BW)], waves.at[:, pl.ds(BW, NB - BW)]),
@@ -164,7 +170,7 @@
     loads = [pltpu.make_async_copy(s, d, load_sems.at[i]) for i, (s, d) in enumerate(loads)]
     for load in loads:
         load.start()
-    lax.fori_loop(0, NDEV - 1, greet, 0, unroll=5)
+    each_other(p, q, greet)
 
     lane = lax.broadcasted_iota(jnp.int32, (1, NG), 1)
 
@@ -188,6 +194,19 @@
     sphere = jnp.concatenate(spheres, axis=1)
     kinetic = jnp.concatenate(kinetics, axis=1)
 
+    cosine = tables[0]
+    sine = tables[1]
+    for i, lower in enumerate((sine, -sine)):
+        table = jnp.concatenate(
+            [
+                jnp.concatenate([cosine, -lower], axis=1),
+                jnp.concatenate([lower, cosine], axis=1),
+            ]
+        )
+        high, low = split(table)
+        mats[2 * i] = high
+        mats[2 * i + 1] = low
+
     psi_re = waves[0, 0:BW, :] * sphere
     psi_im = waves[1, 0:BW, :] * sphere
     rows = []
@@ -217,17 +236,16 @@
 
     loads[5].wait()
     for y in range(4):
-        pot_send[:, y, :] = pot[:, y, :].T
+        pot_send[:, y, :] = pot[y]
 
     pl.semaphore_wait(barrier, NDEV - 1)
 
-    def send_forward(k, carry):
-        to_p, to_q = partner(k, p, q)
-        row = lax.rem(to_p, 2) * NG + to_q * 16 + lax.div(to_p, 2)
+    def send_forward(to_z, to_y, to_core, to_q):
+        to_p = to_z * 4 + (to_y * 2 + to_core)
+        row = to_z * 2 + (to_core * NG + to_q * 16 + to_y)
         remote(fwd_send.at[row], fwd_recv.at[slot], fwd_sems, (to_p, to_q)).start()
-        return carry
-
-    lax.fori_loop(0, NDEV - 1, send_forward, 0, unroll=5)
+
+    each_other(p, q, send_forward)
     own_forward = pltpu.make_async_copy(fwd_send.at[owner], fwd_recv.at[slot], own_sems.at[0])
     own_forward.start()
 
@@ -260,10 +278,16 @@
     own_ca.start()
 
     loads[6].wait()
-    blk_row = lax.broadcasted_iota(jnp.int32, (8, NB), 0)
-    blk_lane = lax.broadcasted_iota(jnp.int32, (8, NB), 1)
-    spread = jnp.where(lax.rem(blk_lane, 8) == blk_row, 1.0, 0.0).astype(F32)
-    wide = jnp.dot(coup[...], spread, precision=lax.Precision.HIGHEST, preferred_element_type=F32)
+    pick_row = lax.broadcasted_iota(jnp.int32, (32, NB), 0)
+    pick_lane = lax.broadcasted_iota(jnp.int32, (32, NB), 1)
+    pick = jnp.where(lax.div(pick_lane, 8) == pick_row, 1.0, 0.0).astype(F32)
+    wide = jnp.dot(
+        coup[...].reshape(64, 32), pick, precision=lax.Precision.HIGHEST, preferred_element_type=F32
+    )
+    blk_j = lax.broadcasted_iota(jnp.int32, (8, 8, NB), 1)
+    blk_lane = lax.broadcasted_iota(jnp.int32, (8, 8, NB), 2)
+    wide = jnp.where(lax.rem(blk_lane, 8) == blk_j, wide.reshape(8, 8, NB), 0.0)
+    wide = jnp.concatenate([jnp.sum(wide, axis=1)] * 32)
     sym_row = lax.broadcasted_iota(jnp.int32, (NB, NB), 0)
     sym_lane = lax.broadcasted_iota(jnp.int32, (NB, NB), 1)
     wide = jnp.where(lax.div(sym_row, 8) == lax.div(sym_lane, 8), wide, 0.0)
@@ -327,14 +351,12 @@
         block = turned[0:32] + turned[32:64] + turned[64:96] + turned[96:128]
         back_send[s * NPX : s * NPX + NPX, 0, :] = block + proj_row
 
-    def send_back(k, carry):
-        to_p, to_q = partner(k, p, q)
-        remote(
-            back_send.at[to_q * NPX + to_p], back_recv.at[owner], back_sems, (to_p, to_q)
-        ).start()
-        return carry
-
-    lax.fori_loop(0, NDEV - 1, send_back, 0, unroll=5)
+    def send_back(to_z, to_y, to_core, to_q):
+        to_p = to_z * 4 + (to_y * 2 + to_core)
+        row = to_z * 4 + (to_q * NPX + to_y * 2 + to_core)
+        remote(back_send.at[row], back_recv.at[owner], back_sems, (to_p, to_q)).start()
+
+    each_other(p, q, send_back)
     own_back = pltpu.make_async_copy(back_send.at[slot], back_recv.at[owner], own_sems.at[3])
     own_back.start()
 
@@ -410,14 +432,12 @@
             block = jnp.where(lax.div(lane, 16) == m, strip, block)
         en_send[h * NPX : h * NPX + NPX, 0, :] = block
 
-    def send_energy(k, carry):
-        to_p, to_q = partner(k, p, q)
-        remote(
-            en_send.at[lax.div(to_q, 4) * NPX + to_p], en_recv.at[slot], en_sems, (to_p, to_q)
-        ).start()
-        return carry
-
-    lax.fori_loop(0, NDEV - 1, send_energy, 0, unroll=5)
+    def send_energy(to_z, to_y, to_core, to_q):
+        to_p = to_z * 4 + (to_y * 2 + to_core)
+        row = to_z * 4 + (lax.div(to_q, 4) * NPX + to_y * 2 + to_core)
+        remote(en_send.at[row], en_recv.at[slot], en_sems, (to_p, to_q)).start()
+
+    each_other(p, q, send_energy)
     own_en = pltpu.make_async_copy(
         en_send.at[lax.div(q, 4) * NPX + p], en_recv.at[slot], own_sems.at[5]
     )
@@ -443,7 +463,7 @@
         n_first = part * 8 + lax.rem(q, 4) * 2
         for n in range(2):
             one = jnp.where(lax.rem(m_lane, 16) == n_first + n, mine, 0.0)
-            energy_ref[part, :, n : n + 1] = jnp.sum(one, axis=1, keepdims=True)
+            energy_ref[part, n : n + 1, :] = jnp.sum(one, axis=1)[None]
 
     wait_bytes(fwd_send.at[pl.ds(0, NDEV - 1)], fwd_sems.at[0])
     wait_bytes(pot_recv.at[pl.ds(0, NPX - 1)], pot_sems.at[0])
@@ -455,23 +475,24 @@
 
 def body(waves, col_map, potential, projectors, coupling):
     vmem = pltpu.VMEM
-    anywhere = pl.BlockSpec(memory_space=pl.ANY)
+    outside = pl.BlockSpec(memory_space=pltpu.HBM)
     inside = pl.BlockSpec(memory_space=pltpu.VMEM)
     mats = jnp.asarray(dft_tables())
-    return pl.pallas_call(
+    hpsi, corr, energy = pl.pallas_call(
         kernel,
         out_shape=(
             jax.ShapeDtypeStruct((2, BW, LOCAL), F32),
             jax.ShapeDtypeStruct((2, 8, 32), F32),
-            jax.ShapeDtypeStruct((2, 8, 2), F32),
+            jax.ShapeDtypeStruct((2, 2, 8), F32),
         ),
-        in_specs=[anywhere] * 6,
+        in_specs=[outside] * 6,
         out_specs=(inside, inside, inside),
         scratch_shapes=[
             vmem((2, NB, LOCAL), F32),
             vmem((2, NB, LOCAL), F32),
-            vmem((NG, 4, 16), F32),
-            vmem((NB, 8), F32),
+            vmem((4, 16, NG), F32),
+            vmem((8, 8, 32), F32),
+            vmem((2, NG, NG), F32),
             vmem((4, 256, 256), BF16),
             pltpu.SMEM((NCOLD,), jnp.int32),
             vmem((2, NB, 2 * LOCAL), BF16),
@@ -504,10 +525,18 @@
             pltpu.SemaphoreType.DMA((2,)),
         ],
         compiler_params=pltpu.CompilerParams(
-            collective_id=0, has_side_effects=True, vmem_limit_bytes=40 << 20
+            collective_id=0, has_side_effects=True, vmem_limit_bytes=60 << 20
         ),
         name="hamiltonian",
-    )(waves, col_map, potential, projectors, coupling.reshape(NB, 8), mats)
+    )(
+        waves,
+        col_map,
+        jnp.transpose(potential, (1, 2, 0)),
+        projectors,
+        jnp.transpose(coupling, (1, 2, 0)),
+        mats,
+    )
+    return hpsi, corr, jnp.transpose(energy, (0, 2, 1))
 
 
 def solution(mesh):

time: 77.9 us -> 47.5 us (0.61)
  Pallas kernels: 70.1 us -> 44 us
  local copies, waits for them, and re-layouts: 6.89 us -> 2.73 us
    pallas_call x1, Pallas kernels: 70.1 us -> 44 us  [body(): pl.pallas_call(kernel, out_shape=(jax.ShapeDtypeStruct((2, BW, LOCAL), F3...]
    unnamed x14 -> x7, local copies, waits for them, and re-layouts: 6.23 us -> 2.73 us
where the time goes in v2:
time: 47.5 us; the launch traced here: 47.4 us
  Pallas kernels  44 us (93%)
  local copies, waits for them, and re-layouts  2.73 us (6%)
  between operations  0.65 us (1%)
    pallas_call x1, Pallas kernels, body(): pl.pallas_call(kernel, out_shape=(jax.ShapeDtypeStruct((2, BW, LOCAL), F3...  44 us
    unnamed x7, local copies, waits for them, and re-layouts  2.73 us

profile of v2, /device:TPU:1, one launch (start us, length us, event | category | flops | bytes accessed | tf_op | source)
XLA Modules:
  0.0 47.4 jit_solution(13316909941217421297)
XLA Ops:
  0.6 44.0 %hamiltonian.1 = (f32[2,16,512]{2,1,0:T(8,128)}, f32[2,8,32]{2,1,0:T(8,128)}, f32[2,2,8]{2,1,0:T(2,128)}) custom-call(f32[2,256,512]{2,1,0:T(8,128)} %waves_hbm.1, s32[4]{0:T(128)} %col_hbm.1, f32[4,16,128]{2,1,0:T(8,128)} %bitcast.3, f32[2,256,512]{2,1,0:T(8,128)} %beta_hbm.1, f32[8,8,32]{2,1,0:T(8,128)} %bitcast.4, f32[2,128,128]{2,1,0:T(8,128)} %constant.2.clone.mats_hbm), custom_call_target="tpu_custom_call" | custom-call | tf_op jit(solution)/shard_map/hamiltonian/pallas_call | solution.py:481
  44.7 0.0 copy-start
  44.7 1.5 %copy.12 = f32[2,16,512]{2,1,0:T(8,128)} copy(f32[2,16,512]{2,1,0:T(8,128)} %get-tuple-element.12) | data formatting | bytes 131072
  46.1 0.0 copy-done
  46.1 0.0 copy-start.1
  46.1 0.6 %copy.13 = f32[2,8,32]{2,1,0:T(8,128)} copy(f32[2,8,32]{2,1,0:T(8,128)S(1)} %copy-done) | data formatting | bytes 4096
  46.7 0.1 copy-done.1
  46.8 0.6 %copy.14 = f32[2,8,2]{1,2,0:T(2,128)} copy(f32[2,8,2]{1,2,0:T(2,128)S(1)} %bitcast.5) | data formatting | bytes 256
Async XLA Ops:
  44.7 1.5 %copy-start = (f32[2,8,32]{2,1,0:T(8,128)S(1)}, f32[2,8,32]{2,1,0:T(8,128)}, u32[]{:S(2)}) copy-start(f32[2,8,32]{2,1,0:T(8,128)} %get-tuple-element.13) | copy-start | bytes 6148
  46.1 0.7 %copy-start.1 = (f32[2,2,8]{2,1,0:T(2,128)S(1)}, f32[2,2,8]{2,1,0:T(2,128)}, u32[]{:S(2)}) copy-start(f32[2,2,8]{2,1,0:T(2,128)} %get-tuple-element.8) | copy-start | bytes 388

commit v3 on v2

--- a/solution.py
+++ b/solution.py
@@ -34,16 +34,19 @@
 
 
 def product(a, b, transposed=False):
+    left = jnp.concatenate([a[0], a[0], a[1]], axis=1)
+    right = jnp.concatenate([b[0], b[1], b[0]], axis=1 if transposed else 0)
     dims = (((1,), (1 if transposed else 0,)), ((), ()))
-
-    def dot(u, v):
-        return lax.dot_general(u, v, dims, preferred_element_type=F32)
-
-    return dot(a[0], b[0]) + (dot(a[0], b[1]) + dot(a[1], b[0]))
+    return lax.dot_general(left, right, dims, preferred_element_type=F32)
 
 
 def pair(ref, *index):
     return ref[(0, *index)], ref[(1, *index)]
+
+
+def store(ref, row, parts):
+    for i, part in enumerate(parts):
+        ref[i, row : row + part.shape[0], :] = part
 
 
 def far_first(digit, half):
@@ -118,7 +121,7 @@
     col,
     phi_s,
     beta_s,
-    sym_s,
+    mixed_s,
     fwd_send,
     fwd_recv,
     pot_send,
@@ -136,6 +139,8 @@
     grid,
     picked,
     ham,
+    lines_s,
+    real_s,
     load_sems,
     own_sems,
     fwd_sems,
@@ -292,8 +297,9 @@
     sym_lane = lax.broadcasted_iota(jnp.int32, (NB, NB), 1)
     wide = jnp.where(lax.div(sym_row, 8) == lax.div(sym_lane, 8), wide, 0.0)
     high, low = split(0.5 * (wide + wide.T))
-    sym_s[0] = high
-    sym_s[1] = low
+    for part in range(2):
+        rows = slice(part * NB, part * NB + NB)
+        store(mixed_s, part * NB, split(product((high, low), pair(beta_s, rows))))
     picked[...] = jnp.zeros((NPY * NG, NG), F32)
 
     own_forward.wait()
@@ -323,23 +329,31 @@
     wait_bytes(pot_recv.at[pl.ds(0, NPX - 1)], pot_sems.at[1])
     potential = pot_recv[...].reshape(NG, NG)
     potential = jnp.concatenate([potential, potential], axis=1)
+    potential = jnp.concatenate([potential, potential])
     mat_a = pair(mats.at[pl.ds(0, 2)])
     mat_b = pair(mats.at[pl.ds(2, 2)])
     for c in range(4):
         two = slice(c * 256, c * 256 + 256)
         lines = product(mat_a, split(field[:, two]))
-        planes = []
         for b in range(2):
             part = lines[:, b * NG : b * NG + NG]
-            planes.append(jnp.concatenate([part[:NG], part[NG:]], axis=1))
-        real = product(split(jnp.concatenate(planes)), mat_b)
-        real = real * jnp.concatenate([potential, potential])
-        back = product(split(real), mat_a)
+            row = (2 * c + b) * NG
+            store(lines_s, row, split(jnp.concatenate([part[:NG], part[NG:]], axis=1)))
+    for c in range(4):
+        two = slice(c * 256, c * 256 + 256)
+        real = product(pair(lines_s, two), mat_b) * potential
+        store(real_s, c * 256, split(real))
+    for c in range(4):
+        two = slice(c * 256, c * 256 + 256)
+        back = product(pair(real_s, two), mat_a)
         columns = []
         for b in range(2):
             part = back[b * NG : b * NG + NG]
             columns.append(jnp.concatenate([part[:, :NG], part[:, NG:]]))
-        grid[:, two] = product(mat_b, split(jnp.concatenate(columns, axis=1)))
+        store(lines_s, c * 256, split(jnp.concatenate(columns, axis=1)))
+    for c in range(4):
+        two = slice(c * 256, c * 256 + 256)
+        grid[:, two] = product(mat_b, pair(lines_s, two))
     for b in range(8):
         for part in range(2):
             plane = grid[part * NG : part * NG + NG, b * NG : b * NG + NG].reshape(16, NPY, NG)
@@ -398,16 +412,15 @@
 
     proj = jnp.concatenate([low_rows, high_rows])
     proj = pltpu.roll(proj, 64, 1).T[0:32]
-    coef = product(split(proj), pair(sym_s))
-    coef_re = coef[0:16]
-    coef_im = coef[16:32]
-    coef = jnp.concatenate(
+    proj_re = proj[0:16]
+    proj_im = proj[16:32]
+    proj = jnp.concatenate(
         [
-            jnp.concatenate([coef_re, -coef_im], axis=1),
-            jnp.concatenate([coef_im, coef_re], axis=1),
+            jnp.concatenate([proj_re, -proj_im], axis=1),
+            jnp.concatenate([proj_im, proj_re], axis=1),
         ]
     )
-    nonlocal_part = product(split(coef), pair(beta_s))
+    nonlocal_part = product(split(proj), pair(mixed_s))
     psi_re = waves[0, 0:BW, :] * sphere
     psi_im = waves[1, 0:BW, :] * sphere
     hpsi_re = kinetic * psi_re + sphere * jnp.concatenate(local_re) + nonlocal_part[0:16]
@@ -473,18 +486,36 @@
     wait_bytes(en_recv.at[pl.ds(0, NDEV - 1)], en_sems.at[0])
 
 
+def finish(hpsi, corr, energy, hpsi_out, corr_out, energy_out, sems):
+    pairs = ((hpsi, hpsi_out), (corr, corr_out), (energy, energy_out))
+    copies = [pltpu.make_async_copy(a, b, sems.at[i]) for i, (a, b) in enumerate(pairs)]
+    for copy in copies:
+        copy.start()
+    for copy in copies:
+        copy.wait()
+
+
 def body(waves, col_map, potential, projectors, coupling):
     vmem = pltpu.VMEM
+    inside = pl.BlockSpec(memory_space=pltpu.VMEM)
     outside = pl.BlockSpec(memory_space=pltpu.HBM)
-    inside = pl.BlockSpec(memory_space=pltpu.VMEM)
     mats = jnp.asarray(dft_tables())
-    hpsi, corr, energy = pl.pallas_call(
+    shapes = (
+        jax.ShapeDtypeStruct((2, BW, LOCAL), F32),
+        jax.ShapeDtypeStruct((2, 8, 32), F32),
+        jax.ShapeDtypeStruct((2, 2, 8), F32),
+    )
+    arrays = (
+        waves,
+        col_map,
+        jnp.transpose(potential, (1, 2, 0)),
+        projectors,
+        jnp.transpose(coupling, (1, 2, 0)),
+        mats,
+    )
+    results = pl.pallas_call(
         kernel,
-        out_shape=(
-            jax.ShapeDtypeStruct((2, BW, LOCAL), F32),
-            jax.ShapeDtypeStruct((2, 8, 32), F32),
-            jax.ShapeDtypeStruct((2, 2, 8), F32),
-        ),
+        out_shape=tuple(vmem(x.shape, x.dtype) for x in shapes),
         in_specs=[outside] * 6,
         out_specs=(inside, inside, inside),
         scratch_shapes=[
@@ -497,7 +528,7 @@
             pltpu.SMEM((NCOLD,), jnp.int32),
             vmem((2, NB, 2 * LOCAL), BF16),
             vmem((2, 2 * NB, LOCAL), BF16),
-            vmem((2, NB, NB), BF16),
+            vmem((2, 2 * NB, LOCAL), BF16),
             vmem((NDEV, 1, NG), F32),
             vmem((NDEV, 1, NG), F32),
             vmem((16, 4, NG), F32),
@@ -515,6 +546,8 @@
             vmem((2 * NG, 8 * NG), F32),
             vmem((NPY * NG, NG), F32),
             vmem((NB, NG), F32),
+            vmem((2, 8 * NG, 256), BF16),
+            vmem((2, 8 * NG, 256), BF16),
             pltpu.SemaphoreType.DMA((7,)),
             pltpu.SemaphoreType.DMA((6,)),
             pltpu.SemaphoreType.DMA((2,)),
@@ -525,17 +558,18 @@
             pltpu.SemaphoreType.DMA((2,)),
         ],
         compiler_params=pltpu.CompilerParams(
-            collective_id=0, has_side_effects=True, vmem_limit_bytes=60 << 20
+            collective_id=0, has_side_effects=True, vmem_limit_bytes=40 << 20
         ),
         name="hamiltonian",
-    )(
-        waves,
-        col_map,
-        jnp.transpose(potential, (1, 2, 0)),
-        projectors,
-        jnp.transpose(coupling, (1, 2, 0)),
-        mats,
-    )
+    )(*(pltpu.with_memory_space_constraint(x, pltpu.HBM) for x in arrays))
+    hpsi, corr, energy = pl.pallas_call(
+        finish,
+        out_shape=shapes,
+        in_specs=[inside] * 3,
+        out_specs=(outside, outside, outside),
+        scratch_shapes=[pltpu.SemaphoreType.DMA((3,))],
+        name="finish",
+    )(*(pltpu.with_memory_space_constraint(x, pltpu.VMEM) for x in results))
     return hpsi, corr, jnp.transpose(energy, (0, 2, 1))
 
 

time: 47.5 us -> 42.8 us (0.901)
  local copies, waits for them, and re-layouts: 2.73 us -> 0 us
  Pallas kernels: 44 us -> 42.1 us
    unnamed x7 -> x0, local copies, waits for them, and re-layouts: 2.73 us -> none
    pallas_call x1 -> x2, Pallas kernels: 44 us -> 42.1 us  [the longest x1 41.4 us: body(): pl.pallas_call(kernel, out_shape=tuple((vmem(x.shape, x.dtype) for x in s...]
where the time goes in v3:
time: 42.8 us; the launch traced here: 42.7 us
  Pallas kernels  42.1 us (98%)
  between operations  0.64 us (1%)
    pallas_call x1, Pallas kernels, body(): pl.pallas_call(kernel, out_shape=tuple((vmem(x.shape, x.dtype) for x in s...  41.4 us

profile of v3, /device:TPU:1, one launch (start us, length us, event | category | flops | bytes accessed | tf_op | source)
XLA Modules:
  0.0 42.7 jit_solution(854424742109872990)
XLA Ops:
  0.6 41.4 %hamiltonian.1 = (f32[2,16,512]{2,1,0:T(8,128)S(1)}, f32[2,8,32]{2,1,0:T(8,128)S(1)}, f32[2,2,8]{2,1,0:T(2,128)S(1)}) custom-call(f32[2,256,512]{2,1,0:T(8,128)} %waves_hbm.1, s32[4]{0:T(128)} %col_hbm.1, f32[4,16,128]{2,1,0:T(8,128)} %bitcast.3, f32[2,256,512]{2,1,0:T(8,128)} %beta_hbm.1, f32[8,8,32]{2,1,0:T(8,128)} %bitcast.4, ...), custom_call_target="tpu_custom_call" | custom-call | tf_op jit(solution)/shard_map/hamiltonian/pallas_call | solution.py:516
  42.0 0.7 %finish.1 = (f32[2,16,512]{2,1,0:T(8,128)}, f32[2,8,32]{2,1,0:T(8,128)}, f32[2,2,8]{2,1,0:T(2,128)}) custom-call(f32[2,16,512]{2,1,0:T(8,128)S(1)} %get-tuple-element.9.hpsi, f32[2,8,32]{2,1,0:T(8,128)S(1)} %get-tuple-element.10.corr, f32[2,2,8]{2,1,0:T(2,128)S(1)} %get-tuple-element.11.energy), custom_call_target="tpu_custom_call" | custom-call | tf_op jit(solution)/shard_map/finish/pallas_call | solution.py:565

commit v4 on v3

--- a/solution.py
+++ b/solution.py
@@ -71,20 +71,18 @@
     z = lax.div(p, 4)
     y_lo = lax.rem(lax.div(p, 2), 2)
     core = lax.rem(p, 2)
-    near = [(1 - y_lo, 1 - core), (1 - y_lo, core), (y_lo, 1 - core), (y_lo, core)]
-    across = [partner_py(jnp.int32(k), q) for k in range(NPY)]
-
-    def level(digit, carry):
-        to_z = lax.rem(z + far_first(digit, 4), 8)
-        for to_q in across:
-            for to_y, to_core in near:
-                visit(to_z, to_y, to_core, to_q)
-        return carry
-
-    lax.fori_loop(0, 7, level, 0)
-    others = [(to_y, to_core, to_q) for to_q in across for to_y, to_core in near]
-    for to_y, to_core, to_q in others[:-1]:
-        visit(z, to_y, to_core, to_q)
+    x = lax.div(q, 2)
+    y_hi = lax.rem(q, 2)
+    to_z = [lax.rem(z + d, 8) for d in range(8)]
+    to_y = [y_lo, 1 - y_lo]
+    to_core = [core, 1 - core]
+    to_q = [[lax.rem(x + d, 4) * 2 + h for h in (y_hi, 1 - y_hi)] for d in range(4)]
+    hops = []
+    for dz, dx, hi, lo, dc in np.ndindex(8, 4, 2, 2, 2):
+        far = min(dz, 8 - dz) + min(dx, 4 - dx) + (1 if lo else 2 * hi) + 0.6 * dc
+        hops.append((-far, dz, dx, hi, lo, dc))
+    for _, dz, dx, hi, lo, dc in sorted(hops)[:-1]:
+        visit(to_z[dz], to_y[lo], to_core[dc], to_q[dx][hi])
 
 
 def remote(src, dst, sems, place):

time: 42.8 us -> 41.2 us (0.963)
  Pallas kernels: 42.1 us -> 40.5 us
    pallas_call x1, Pallas kernels: 41.4 us -> 39.8 us  [body(): pl.pallas_call(kernel, out_shape=tuple((vmem(x.shape, x.dtype) for x in s...]
where the time goes in v4:
time: 41.2 us; the launch traced here: 41.1 us
  Pallas kernels  40.5 us (98%)
  between operations  0.64 us (2%)
    pallas_call x1, Pallas kernels, body(): pl.pallas_call(kernel, out_shape=tuple((vmem(x.shape, x.dtype) for x in s...  39.8 us

profile of v4, /device:TPU:1, one launch (start us, length us, event | category | flops | bytes accessed | tf_op | source)
XLA Modules:
  0.0 41.1 jit_solution(1138465392052061161)
XLA Ops:
  0.6 39.8 %hamiltonian.1 = (f32[2,16,512]{2,1,0:T(8,128)S(1)}, f32[2,8,32]{2,1,0:T(8,128)S(1)}, f32[2,2,8]{2,1,0:T(2,128)S(1)}) custom-call(f32[2,256,512]{2,1,0:T(8,128)} %waves_hbm.1, s32[4]{0:T(128)} %col_hbm.1, f32[4,16,128]{2,1,0:T(8,128)} %bitcast.3, f32[2,256,512]{2,1,0:T(8,128)} %beta_hbm.1, f32[8,8,32]{2,1,0:T(8,128)} %bitcast.4, ...), custom_call_target="tpu_custom_call" | custom-call | tf_op jit(solution)/shard_map/hamiltonian/pallas_call | solution.py:514
  40.4 0.7 %finish.1 = (f32[2,16,512]{2,1,0:T(8,128)}, f32[2,8,32]{2,1,0:T(8,128)}, f32[2,2,8]{2,1,0:T(2,128)}) custom-call(f32[2,16,512]{2,1,0:T(8,128)S(1)} %get-tuple-element.9.hpsi, f32[2,8,32]{2,1,0:T(8,128)S(1)} %get-tuple-element.10.corr, f32[2,2,8]{2,1,0:T(2,128)S(1)} %get-tuple-element.11.energy), custom_call_target="tpu_custom_call" | custom-call | tf_op jit(solution)/shard_map/finish/pallas_call | solution.py:563

commit v5 on v4

--- a/solution.py
+++ b/solution.py
@@ -235,7 +235,7 @@
     for h in range(2):
         part = pltpu.roll(z_rows, 64, 1) if h else z_rows
         rows = jnp.where(lane < 64, part, partial[h * NG : h * NG + NG]) + cols
-        fwd_send[h * NG : h * NG + NG, 0, :] = rows
+        fwd_send[h * NG : h * NG + NG, :] = rows
 
     loads[5].wait()
     for y in range(4):
@@ -246,10 +246,10 @@
     def send_forward(to_z, to_y, to_core, to_q):
         to_p = to_z * 4 + (to_y * 2 + to_core)
         row = to_z * 2 + (to_core * NG + to_q * 16 + to_y)
-        remote(fwd_send.at[row], fwd_recv.at[slot], fwd_sems, (to_p, to_q)).start()
+        remote(fwd_send.at[pl.ds(row, 1)], fwd_recv.at[pl.ds(slot, 1)], fwd_sems, (to_p, to_q)).start()
 
     each_other(p, q, send_forward)
-    own_forward = pltpu.make_async_copy(fwd_send.at[owner], fwd_recv.at[slot], own_sems.at[0])
+    own_forward = pltpu.make_async_copy(fwd_send.at[pl.ds(owner, 1)], fwd_recv.at[pl.ds(slot, 1)], own_sems.at[0])
     own_forward.start()
 
     def send_potential(k, carry):
@@ -304,7 +304,7 @@
     wait_bytes(fwd_recv.at[pl.ds(0, NDEV - 1)], fwd_sems.at[1])
     proj_sum = jnp.zeros((NPX, NG), F32)
     for s in range(NPY):
-        block = fwd_recv[s * NPX : s * NPX + NPX, 0, :]
+        block = fwd_recv[s * NPX : s * NPX + NPX, :]
         proj_sum = proj_sum + block
         unpack[s * NG : s * NG + NG, :] = jnp.concatenate([block] * 4).T
     proj_sum = jnp.sum(proj_sum, axis=0, keepdims=True)
@@ -361,15 +361,15 @@
     for s in range(NPY):
         turned = picked[s * NG : s * NG + NG, :].T
         block = turned[0:32] + turned[32:64] + turned[64:96] + turned[96:128]
-        back_send[s * NPX : s * NPX + NPX, 0, :] = block + proj_row
+        back_send[s * NPX : s * NPX + NPX, :] = block + proj_row
 
     def send_back(to_z, to_y, to_core, to_q):
         to_p = to_z * 4 + (to_y * 2 + to_core)
         row = to_z * 4 + (to_q * NPX + to_y * 2 + to_core)
-        remote(back_send.at[row], back_recv.at[owner], back_sems, (to_p, to_q)).start()
+        remote(back_send.at[pl.ds(row, 1)], back_recv.at[pl.ds(owner, 1)], back_sems, (to_p, to_q)).start()
 
     each_other(p, q, send_back)
-    own_back = pltpu.make_async_copy(back_send.at[slot], back_recv.at[owner], own_sems.at[3])
+    own_back = pltpu.make_async_copy(back_send.at[pl.ds(slot, 1)], back_recv.at[pl.ds(owner, 1)], own_sems.at[3])
     own_back.start()
 
     own_ca.wait()
@@ -392,8 +392,8 @@
 
     own_back.wait()
     wait_bytes(back_recv.at[pl.ds(0, NDEV - 1)], back_sems.at[1])
-    low_rows = back_recv[0:NG, 0, :]
-    high_rows = back_recv[NG : 2 * NG, 0, :]
+    low_rows = back_recv[0:NG, :]
+    high_rows = back_recv[NG : 2 * NG, :]
     lines = jnp.where(lane < 64, low_rows, pltpu.roll(high_rows, 64, 1)).T
     lines = product(split(lines), pair(mats.at[pl.ds(2, 2)], slice(0, NG)))
     local_re = []
@@ -418,7 +418,11 @@
             jnp.concatenate([proj_im, proj_re], axis=1),
         ]
     )
-    nonlocal_part = product(split(proj), pair(mixed_s))
+    high, low = split(proj)
+    mixed = pair(mixed_s)
+    stacked = jnp.dot(jnp.concatenate([high, low]), mixed[0], preferred_element_type=F32)
+    nonlocal_part = jnp.dot(high, mixed[1], preferred_element_type=F32)
+    nonlocal_part = stacked[0:32] + stacked[32:64] + nonlocal_part
     psi_re = waves[0, 0:BW, :] * sphere
     psi_im = waves[1, 0:BW, :] * sphere
     hpsi_re = kinetic * psi_re + sphere * jnp.concatenate(local_re) + nonlocal_part[0:16]
@@ -432,25 +436,29 @@
         im = hpsi_im[h * 8 : h * 8 + 8]
         rows.append(jnp.concatenate([re, im], axis=1))
         rows.append(jnp.concatenate([im, -re], axis=1))
-    rows = split(jnp.concatenate(rows))
-    rows = tuple(jnp.concatenate([x[0:16]] * 8 + [x[16:32]] * 8) for x in rows)
-    partial = product(pair(phi_s), rows, True)
+    high, low = split(jnp.concatenate(rows))
+    phi = pair(phi_s)
+    dims = (((1,), (1,)), ((), ()))
+    both = jnp.concatenate([high, low, jnp.zeros((64, 2 * LOCAL), BF16)])
+    both = lax.dot_general(phi[0], both, dims, preferred_element_type=F32)
+    high = jnp.concatenate([high, jnp.zeros((96, 2 * LOCAL), BF16)])
+    rest = lax.dot_general(phi[1], high, dims, preferred_element_type=F32)
+    ham[...] = both + pltpu.roll(both, 96, 1) + rest
     for h in range(2):
-        ham[...] = partial[:, h * NG : h * NG + NG]
         block = jnp.zeros((NPX, NG), F32)
         for m in range(8):
-            strip = ham[pl.ds(m, NPX, stride=8), :]
+            strip = pltpu.roll(ham[pl.ds(m, NPX, stride=8), :], (m - h) * 16 % NG, 1)
             block = jnp.where(lax.div(lane, 16) == m, strip, block)
-        en_send[h * NPX : h * NPX + NPX, 0, :] = block
+        en_send[h * NPX : h * NPX + NPX, :] = block
 
     def send_energy(to_z, to_y, to_core, to_q):
         to_p = to_z * 4 + (to_y * 2 + to_core)
         row = to_z * 4 + (lax.div(to_q, 4) * NPX + to_y * 2 + to_core)
-        remote(en_send.at[row], en_recv.at[slot], en_sems, (to_p, to_q)).start()
+        remote(en_send.at[pl.ds(row, 1)], en_recv.at[pl.ds(slot, 1)], en_sems, (to_p, to_q)).start()
 
     each_other(p, q, send_energy)
     own_en = pltpu.make_async_copy(
-        en_send.at[lax.div(q, 4) * NPX + p], en_recv.at[slot], own_sems.at[5]
+        en_send.at[pl.ds(lax.div(q, 4) * NPX + p, 1)], en_recv.at[pl.ds(slot, 1)], own_sems.at[5]
     )
     own_en.start()
 
@@ -465,7 +473,7 @@
     wait_bytes(en_recv.at[pl.ds(0, NDEV - 1)], en_sems.at[1])
     total = jnp.zeros((NPX, NG), F32)
     for s in range(NPY):
-        total = total + en_recv[s * NPX : s * NPX + NPX, 0, :]
+        total = total + en_recv[s * NPX : s * NPX + NPX, :]
     total = jnp.sum(total, axis=0, keepdims=True) * scale
     m_row = lax.broadcasted_iota(jnp.int32, (8, NG), 0)
     m_lane = lax.broadcasted_iota(jnp.int32, (8, NG), 1)
@@ -527,18 +535,18 @@
             vmem((2, NB, 2 * LOCAL), BF16),
             vmem((2, 2 * NB, LOCAL), BF16),
             vmem((2, 2 * NB, LOCAL), BF16),
-            vmem((NDEV, 1, NG), F32),
-            vmem((NDEV, 1, NG), F32),
+            vmem((NDEV, NG), F32),
+            vmem((NDEV, NG), F32),
             vmem((16, 4, NG), F32),
             vmem((NPX, 4, NG), F32),
             vmem((NPY, 2, 32, NB), F32),
             vmem((NPY, 2, 32, NB), F32),
             vmem((NPX, 8, NG), F32),
             vmem((NPX, 8, NG), F32),
-            vmem((NDEV, 1, NG), F32),
-            vmem((NDEV, 1, NG), F32),
-            vmem((2 * NPX, 1, NG), F32),
-            vmem((NDEV, 1, NG), F32),
+            vmem((NDEV, NG), F32),
+            vmem((NDEV, NG), F32),
+            vmem((2 * NPX, NG), F32),
+            vmem((NDEV, NG), F32),
             vmem((NPY * NG, NG), F32),
             vmem((2 * NG, 8 * NG), F32),
             vmem((2 * NG, 8 * NG), F32),

time: 41.2 us -> 40.6 us (0.985)
  Pallas kernels: 40.5 us -> 39.9 us
    pallas_call x1, Pallas kernels: 39.8 us -> 39.2 us  [body(): pl.pallas_call(kernel, out_shape=tuple((vmem(x.shape, x.dtype) for x in s...]
where the time goes in v5:
time: 40.6 us; the launch traced here: 40.5 us
  Pallas kernels  39.9 us (98%)
  between operations  0.64 us (2%)
    pallas_call x1, Pallas kernels, body(): pl.pallas_call(kernel, out_shape=tuple((vmem(x.shape, x.dtype) for x in s...  39.2 us

profile of v5, /device:TPU:1, one launch (start us, length us, event | category | flops | bytes accessed | tf_op | source)
XLA Modules:
  0.0 40.5 jit_solution(15442573971980072180)
XLA Ops:
  0.6 39.2 %hamiltonian.1 = (f32[2,16,512]{2,1,0:T(8,128)S(1)}, f32[2,8,32]{2,1,0:T(8,128)S(1)}, f32[2,2,8]{2,1,0:T(2,128)S(1)}) custom-call(f32[2,256,512]{2,1,0:T(8,128)} %waves_hbm.1, s32[4]{0:T(128)} %col_hbm.1, f32[4,16,128]{2,1,0:T(8,128)} %bitcast.3, f32[2,256,512]{2,1,0:T(8,128)} %beta_hbm.1, f32[8,8,32]{2,1,0:T(8,128)} %bitcast.4, ...), custom_call_target="tpu_custom_call" | custom-call | tf_op jit(solution)/shard_map/hamiltonian/pallas_call | solution.py:522
  39.9 0.7 %finish.1 = (f32[2,16,512]{2,1,0:T(8,128)}, f32[2,8,32]{2,1,0:T(8,128)}, f32[2,2,8]{2,1,0:T(2,128)}) custom-call(f32[2,16,512]{2,1,0:T(8,128)S(1)} %get-tuple-element.9.hpsi, f32[2,8,32]{2,1,0:T(8,128)S(1)} %get-tuple-element.10.corr, f32[2,2,8]{2,1,0:T(2,128)S(1)} %get-tuple-element.11.energy), custom_call_target="tpu_custom_call" | custom-call | tf_op jit(solution)/shard_map/finish/pallas_call | solution.py:571

commit v6 on v5

--- a/solution.py
+++ b/solution.py
@@ -54,17 +54,23 @@
     return half + (1 - 2 * odd) * lax.div(digit + 1, 2)
 
 
-def partner_px(k, p):
-    z = lax.rem(lax.div(p, 4) + far_first(lax.div(k, 4), 4), 8)
-    y_lo = lax.rem(lax.div(p, 2) + 1 + lax.rem(lax.div(k, 2), 2), 2)
-    core = lax.rem(p + 1 + lax.rem(k, 2), 2)
-    return z * 4 + y_lo * 2 + core
-
-
 def partner_py(k, q):
     x = lax.rem(lax.div(q, 2) + far_first(lax.div(k, 2), 2), 4)
     y_hi = lax.rem(q + 1 + lax.rem(k, 2), 2)
     return x * 2 + y_hi
+
+
+def along_px(p):
+    z = lax.div(p, 4)
+    y_lo = lax.rem(lax.div(p, 2), 2)
+    core = lax.rem(p, 2)
+    to_z = [lax.rem(z + d, 8) for d in range(8)]
+    to_y = [y_lo, 1 - y_lo]
+    to_core = [core, 1 - core]
+    hops = []
+    for dz, lo, dc in np.ndindex(8, 2, 2):
+        hops.append((-(min(dz, 8 - dz) + lo + 0.6 * dc), dz, lo, dc))
+    return [(to_z[dz], to_y[lo], to_core[dc]) for _, dz, lo, dc in sorted(hops)[:-1]]
 
 
 def each_other(p, q, visit):
@@ -252,12 +258,10 @@
     own_forward = pltpu.make_async_copy(fwd_send.at[pl.ds(owner, 1)], fwd_recv.at[pl.ds(slot, 1)], own_sems.at[0])
     own_forward.start()
 
-    def send_potential(k, carry):
-        to_p = partner_px(k, p)
-        remote(pot_send.at[lax.div(to_p, 2)], pot_recv.at[p], pot_sems, (to_p, q)).start()
-        return carry
-
-    lax.fori_loop(0, NPX - 1, send_potential, 0)
+    for to_z, to_y, to_core in along_px(p):
+        row = to_z * 2 + to_y
+        to_p = to_z * 4 + (to_y * 2 + to_core)
+        remote(pot_send.at[row], pot_recv.at[p], pot_sems, (to_p, q)).start()
     own_pot = pltpu.make_async_copy(pot_send.at[z_low], pot_recv.at[p], own_sems.at[1])
     own_pot.start()
 
@@ -381,12 +385,9 @@
     total = jnp.concatenate([total, jnp.zeros((64, NB), F32)])
     cb_send[...] = total.T.reshape(NPX, 8, NG)
 
-    def send_corr_b(k, carry):
-        to_p = partner_px(k, p)
+    for to_z, to_y, to_core in along_px(p):
+        to_p = to_z * 4 + (to_y * 2 + to_core)
         remote(cb_send.at[to_p], cb_recv.at[p], cb_sems, (to_p, q)).start()
-        return carry
-
-    lax.fori_loop(0, NPX - 1, send_corr_b, 0)
     own_cb = pltpu.make_async_copy(cb_send.at[p], cb_recv.at[p], own_sems.at[4])
     own_cb.start()
 

time: 40.6 us -> 40.8 us (level)
  no operation moved by 1% of the time
where the time goes in v6:
time: 40.8 us; the launch traced here: 40.7 us
  Pallas kernels  40.1 us (98%)
  between operations  0.64 us (2%)
    pallas_call x1, Pallas kernels, body(): pl.pallas_call(kernel, out_shape=tuple((vmem(x.shape, x.dtype) for x in s...  39.4 us

profile of v6, /device:TPU:1, one launch (start us, length us, event | category | flops | bytes accessed | tf_op | source)
XLA Modules:
  0.0 40.7 jit_solution(6256088575944553375)
XLA Ops:
  0.6 39.4 %hamiltonian.1 = (f32[2,16,512]{2,1,0:T(8,128)S(1)}, f32[2,8,32]{2,1,0:T(8,128)S(1)}, f32[2,2,8]{2,1,0:T(2,128)S(1)}) custom-call(f32[2,256,512]{2,1,0:T(8,128)} %waves_hbm.1, s32[4]{0:T(128)} %col_hbm.1, f32[4,16,128]{2,1,0:T(8,128)} %bitcast.3, f32[2,256,512]{2,1,0:T(8,128)} %beta_hbm.1, f32[8,8,32]{2,1,0:T(8,128)} %bitcast.4, ...), custom_call_target="tpu_custom_call" | custom-call | tf_op jit(solution)/shard_map/hamiltonian/pallas_call | solution.py:523
  40.0 0.7 %finish.1 = (f32[2,16,512]{2,1,0:T(8,128)}, f32[2,8,32]{2,1,0:T(8,128)}, f32[2,2,8]{2,1,0:T(2,128)}) custom-call(f32[2,16,512]{2,1,0:T(8,128)S(1)} %get-tuple-element.9.hpsi, f32[2,8,32]{2,1,0:T(8,128)S(1)} %get-tuple-element.10.corr, f32[2,2,8]{2,1,0:T(2,128)S(1)} %get-tuple-element.11.energy), custom_call_target="tpu_custom_call" | custom-call | tf_op jit(solution)/shard_map/finish/pallas_call | solution.py:572
